TPU v7x, 512 devices: a whole 4x8x8 slice. The times are simulated.
512 devices in a mesh: dp: 128 (over z, y, core), mp: 4 (over x).
Axes of the slice: x: 4, y: 8, z: 8, core: 2. Of those that a mesh axis runs over, the one named last changes fastest.
Arguments:
- grads: bfloat16 [384, 512, 512], P(None, 'dp', 'mp'), may hold values from -6 to 6
- owner: int32 [384], replicated, may hold values from 0 to 127, as said below
- left_stat: float32 [384, 512, 512], P('dp', 'mp')
- right_stat: float32 [384, 512, 512], P('dp', 'mp')
- left_root: bfloat16 [384, 512, 512], P('dp', 'mp')
- right_root: bfloat16 [384, 512, 512], P('dp', 'mp')
Outputs:
- new_left: float32 [384, 512, 512], P('dp', 'mp')
- new_right: float32 [384, 512, 512], P('dp', 'mp')
- precond: bfloat16 [384, 512, 512], P(None, 'dp', 'mp')
Inputs may be any that keep to these rules, and one draw needn't show every extreme that they name: Every owner index names exactly 3 blocks.
All inputs are finite; a program needn't handle non-finite values.
Results may differ from a plain program's by a relative error of at most 0.0049.
Values may be sent and summed in bfloat16 or wider, within the bound.
A program may use at most 64 MiB of HBM per device.

v0:
```python
import jax
import jax.numpy as jnp
from jax import lax
from jax.sharding import PartitionSpec as P

DECAY = 0.9
EPSILON = 1e-06


def local(grads, owner, left_stat, right_stat, left_root, right_root):
    quarter = left_stat.shape[1]
    block_width = left_stat.shape[2]
    column_part = grads.shape[2]
    member = lax.axis_index("mp")
    slot_order = jnp.argsort(owner, stable=True)
    sorted_pieces = jnp.take(grads, slot_order, axis=0)
    arrived = lax.all_to_all(sorted_pieces, "dp", split_axis=0, concat_axis=1, tiled=True)
    full_grad = lax.all_gather(arrived, "mp", axis=2, tiled=True)
    row_start = member * quarter
    own_rows = lax.dynamic_slice_in_dim(full_grad, row_start, quarter, 1)
    own_columns = lax.dynamic_slice_in_dim(full_grad, row_start, quarter, 2)
    outer_left = jnp.einsum("orb,ocb->orc", own_rows, full_grad, preferred_element_type=jnp.float32)
    outer_right = jnp.einsum(
        "oar,oab->orb", own_columns, full_grad, preferred_element_type=jnp.float32
    )
    new_left = DECAY * left_stat + (1.0 - DECAY) / block_width * outer_left
    new_right = DECAY * right_stat + (1.0 - DECAY) / block_width * outer_right
    full_factor = lax.all_gather(right_root, "mp", axis=1, tiled=True)
    half_way = jnp.einsum(
        "oab,obc->oac", full_grad, full_factor, preferred_element_type=jnp.float32
    ).astype(jnp.bfloat16)
    product = jnp.einsum("orb,obc->orc", left_root, half_way, preferred_element_type=jnp.float32)
    grad_wide = full_grad.astype(jnp.float32)
    grad_squares = jnp.sum(grad_wide * grad_wide, axis=(1, 2))
    product_squares = lax.psum(jnp.sum(product * product, axis=(1, 2)), "mp")
    graft_scale = jnp.sqrt(grad_squares / (product_squares + EPSILON))
    finished = (product * graft_scale[:, None, None]).astype(jnp.bfloat16)
    whole_rows = lax.all_gather(finished, "mp", axis=1, tiled=True)
    column_slice = lax.dynamic_slice_in_dim(whole_rows, member * column_part, column_part, 2)
    returned = lax.all_to_all(column_slice, "dp", split_axis=1, concat_axis=0, tiled=True)
    inverse = jnp.argsort(slot_order)
    precond = jnp.take(returned, inverse, axis=0)
    return (new_left, new_right, precond)


def solution(mesh):
    in_specs = (
        P(None, "dp", "mp"),
        P(),
        P("dp", "mp", None),
        P("dp", "mp", None),
        P("dp", "mp", None),
        P("dp", "mp", None),
    )
    out_specs = (P("dp", "mp", None), P("dp", "mp", None), P(None, "dp", "mp"))
    return jax.shard_map(local, mesh=mesh, in_specs=in_specs, out_specs=out_specs, check_vma=False)
```

profile of v0, /device:TPU:1, one launch (start us, length us, event | category | flops | bytes accessed | tf_op | source)
XLA Modules:
  0.0 183.2 jit_solution(11618610305547093010)
XLA Ops:
  7.2 0.0 copy-start
  7.2 0.0 all-gather.6.cloned.1.call-start
  7.2 0.7 all-gather.6.cloned.1.call-update
  7.9 0.0 all-gather.4.cloned.1.call-start
  8.0 4.4 %sort.34 = (s32[384]{0:T(512)}, s32[384]{0:T(512)S(1)}) sort(s32[384]{0:T(512)} %param.9, s32[384]{0:T(512)S(1)} %iota.8), dimensions={0}, to_apply=%region_0.0 | sort | flops 3456 | bytes 6144 | tf_op jit(solution)/shard_map/jit(argsort)/sort | solution.py:15
  12.4 2.2 %gather_fusion = bf16[384,4,128]{2,1,0:T(4,128)(2,1)S(1)} fusion(bf16[384,4,128]{2,1,0:T(4,128)(2,1)} %param.8, s32[1024]{0:T(1024)S(1)} %pad_clamp_fusion.1), kind=kCustom, calls=%fused_computation.clone | custom fusion | bytes 787968 | tf_op jit(solution)/shard_map/jit(_take)/gather | solution.py:16
  14.7 1.3 broadcast_select_fusion.1
  16.0 36.1 %all_to_all.36 = bf16[384,4,128]{2,1,0:T(4,128)(2,1)S(1)} all-to-all(bf16[384,4,128]{2,1,0:T(4,128)(2,1)S(1)} %broadcast_select_fusion.1), channel_id=1, replica_groups=mesh['dp'=128,'mp'=4] {'dp'}, dimensions={0} | all-to-all | bytes 786432 | tf_op jit(solution)/shard_map/all_to_all | solution.py:17
  52.1 0.9 copy.15
  53.0 0.0 all-gather.4.cloned.1.call-update
  53.0 0.0 all-gather.8.cloned.1.call-start
  53.1 0.0 all-gather.6.cloned.1.call-done
  53.1 31.9 %all-gather.4.cloned.1.call-done = bf16[3,512,512]{2,1,0:T(8,128)(2,1)} async-done(((bf16[3,512,128]{2,1,0:T(8,128)(2,1)}), bf16[3,512,512]{2,1,0:T(8,128)(2,1)}) %all-gather.4.cloned.1.call-update) | async-done | bytes 1572880 | tf_op jit(solution)/shard_map/all_gather | solution.py:18
  85.0 0.0 copy-done
  85.0 0.0 copy-start.1
  85.0 3.5 %multiply_reduce_fusion.1 = (f32[3]{0:T(128)S(1)}, f32[3,512,128]{2,1,0:T(8,128)S(1)}) fusion(bf16[3,128,512]{2,1,0:T(8,128)(2,1)S(1)} %copy-done, bf16[3,512,512]{2,1,0:T(8,128)(2,1)} %all-gather.4.cloned.1.call-done, bf16[3,512,512]{2,1,0:T(8,128)(2,1)} %all-gather.6.cloned.1.call-done), kind=kOutput, calls=%fused_computation.10 | convolution fusion | flops 1007812608 | bytes 4325388 | tf_op jit(solution)/shard_map/orb,obc->orc/dot_general | solution.py:32
  88.5 7.7 %psum.7 = f32[3]{0:T(128)S(1)} all-reduce(f32[3]{0:T(128)S(1)} %get-tuple-element.8), channel_id=1, replica_groups=mesh['dp'=128,'mp'=4] {'mp'}, use_global_device_ids=true, to_apply=%region_3.5 | all-reduce | flops 3 | bytes 24 | tf_op jit(solution)/shard_map/psum | solution.py:35
  96.3 0.0 copy-done.1
  96.3 0.5 multiply_reduce_fusion
  96.8 0.9 fusion.3
  97.7 0.0 copy-start.2
  97.7 0.0 all-gather.8.cloned.1.call-update
  97.7 3.8 %sort.35 = (s32[384]{0:T(512)}, s32[384]{0:T(512)S(1)}) sort(s32[384]{0:T(512)S(1)} %get-tuple-element.6, s32[384]{0:T(512)S(1)} %iota.9), dimensions={0}, to_apply=%region_4.6 | sort | flops 3456 | bytes 6144 | tf_op jit(solution)/shard_map/jit(argsort)/sort | solution.py:41
  101.5 33.1 %all-gather.8.cloned.1.call-done = bf16[3,512,512]{1,2,0:T(8,128)(2,1)} async-done(((bf16[3,128,512]{1,2,0:T(8,128)(2,1)}), bf16[3,512,512]{1,2,0:T(8,128)(2,1)}) %all-gather.8.cloned.1.call-update) | async-done | bytes 1572880 | tf_op jit(solution)/shard_map/all_gather | solution.py:38
  134.6 1.0 constant_dynamic-slice_fusion
  135.6 1.1 copy.18
  136.7 15.2 %all-to-all-start.1 = ((bf16[3,512,128]{2,0,1:T(4,128)(2,1)}), bf16[3,512,128]{2,0,1:T(4,128)(2,1)S(1)}, u32[]{:S(2)}, u32[]{:S(2)}) async-start(bf16[3,512,128]{2,0,1:T(4,128)(2,1)} %copy.18), calls=%async_computation.1 | async-start | bytes 1048576 | tf_op jit(solution)/shard_map/all_to_all | solution.py:40
  151.8 0.0 copy-done.2
  151.9 0.0 copy-start.3
  151.9 1.3 fusion.1
  153.2 0.0 copy-done.3
  153.2 1.5 fusion.2
  154.7 17.7 %all-to-all-done.1 = bf16[3,512,128]{2,0,1:T(4,128)(2,1)S(1)} async-done(((bf16[3,512,128]{2,0,1:T(4,128)(2,1)}), bf16[3,512,128]{2,0,1:T(4,128)(2,1)S(1)}, u32[]{:S(2)}, u32[]{:S(2)}) %all-to-all-start.1) | async-done | bytes 393248 | tf_op jit(solution)/shard_map/all_to_all | solution.py:40
  172.4 0.1 copy.19
  172.5 0.1 copy.20
  172.6 2.0 %gather_fusion.1 = bf16[384,4,128]{2,1,0:T(4,128)(2,1)S(1)} fusion(bf16[384,4,128]{2,1,0:T(4,128)(2,1)S(1)} %bitcast.16, s32[1024]{0:T(1024)S(1)} %pad_clamp_fusion), kind=kCustom, calls=%fused_computation.1.clone | custom fusion | bytes 787968 | tf_op jit(solution)/shard_map/jit(_take)/gather | solution.py:42
  174.7 2.0 %broadcast_select_fusion = bf16[384,4,128]{2,1,0:T(4,128)(2,1)} fusion(bf16[384,4,128]{2,1,0:T(4,128)(2,1)S(1)} %gather_fusion.1, pred[384]{0:T(512)(128)(4,1)S(1)} %compare_and_fusion), kind=kLoop, calls=%fused_computation.14 | loop fusion | flops 196608 | bytes 786816 | tf_op jit(solution)/shard_map/jit(_take)/select_n | solution.py:42
  (9 shorter events, 0.1 us)
Async XLA Ops:
  7.2 77.8 %copy-start = (bf16[3,128,512]{2,1,0:T(8,128)(2,1)S(1)}, bf16[3,128,512]{2,1,0:T(8,128)(2,1)}, u32[]{:S(2)}) copy-start(bf16[3,128,512]{2,1,0:T(8,128)(2,1)} %param.12) | copy-start | bytes 1179652
  7.2 45.9 %all-gather.6.cloned.1.call-start = ((), (), s32[]{:S(2)}) async-start(), calls=%async_computation.3 | async-start | bytes 1966080 | tf_op jit(solution)/shard_map/all_gather | solution.py:28
  7.9 77.1 %all-gather.4.cloned.1.call-start = ((), (), s32[]{:S(2)}) async-start(), calls=%async_computation.2 | async-start | bytes 1966080 | tf_op jit(solution)/shard_map/all_gather | solution.py:18
  53.0 81.6 %all-gather.8.cloned.1.call-start = ((), (), s32[]{:S(2)}) async-start(), calls=%async_computation.4 | async-start | bytes 1966080 | tf_op jit(solution)/shard_map/all_gather | solution.py:38
  85.0 11.3 %copy-start.1 = (bf16[3,512,512]{2,1,0:T(8,128)(2,1)S(1)}, bf16[3,512,512]{2,1,0:T(8,128)(2,1)}, u32[]{:S(2)}) copy-start(bf16[3,512,512]{2,1,0:T(8,128)(2,1)} %all-gather.4.cloned.1.call-done) | copy-start | bytes 4718596
  97.7 54.2 %copy-start.2 = (f32[3,128,512]{2,1,0:T(8,128)S(1)}, f32[3,128,512]{2,1,0:T(8,128)}, u32[]{:S(2)}) copy-start(f32[3,128,512]{2,1,0:T(8,128)} %param.11) | copy-start | bytes 2359300
  136.7 35.7 %all-to-all-start.1 = ((bf16[3,512,128]{2,0,1:T(4,128)(2,1)}), bf16[3,512,128]{2,0,1:T(4,128)(2,1)S(1)}, u32[]{:S(2)}, u32[]{:S(2)}) async-start(bf16[3,512,128]{2,0,1:T(4,128)(2,1)} %copy.18), calls=%async_computation.1 | async-start | bytes 1048576 | tf_op jit(solution)/shard_map/all_to_all | solution.py:40
  151.9 1.3 copy-start.3
Sparse Core Ops, SparseCore 0:
  10.1 37.3 all-gather.5
  53.1 31.8 all-gather.3
  97.8 36.7 all-gather.7
where the time goes:
time: 183 us
  waiting for transfers between devices  83.4 us (46%)
  blocking collectives  43.9 us (24%)
  starting transfers between devices  15.3 us (8%)
  between operations  13.9 us (8%)
  other arithmetic  12.9 us (7%)
  local copies, waits for them, and re-layouts  7.45 us (4%)
  matrix products  6.37 us (3%)
    all_to_all x1, blocking collectives, local(): lax.all_to_all(sorted_pieces, 'dp', split_axis=0, concat_axis=1, tiled=True)  36.1 us
    all_gather x1, waiting for transfers between devices, local(): whole_rows = lax.all_gather(finished, 'mp', axis=1, tiled=True)  33.1 us
    all_gather x1, waiting for transfers between devices, local(): full_grad = lax.all_gather(arrived, 'mp', axis=2, tiled=True)  31.9 us
    all_to_all x1, waiting for transfers between devices, local(): lax.all_to_all(column_slice, 'dp', split_axis=1, concat_axis=0, tiled=True)  17.7 us
    all_to_all x1, starting transfers between devices, local(): lax.all_to_all(column_slice, 'dp', split_axis=1, concat_axis=0, tiled=True)  15.2 us
    psum x1, blocking collectives, local(): product_squares = lax.psum(jnp.sum(product * product, axis=(1, 2)), 'mp')  7.75 us
    sort x1, other arithmetic, local(): slot_order = jnp.argsort(owner, stable=True)  4.45 us
    sort x1, other arithmetic, local(): inverse = jnp.argsort(slot_order)  3.77 us
  transfers between devices with their start and end apart: 4, of which 3 were waited for; matrix products, arithmetic and copies ran while one was open for 8% of the time, Pallas kernels for 0%

commit v1 on v0

v1 whole, which is shorter than its diff:
```python
import jax
import jax.numpy as jnp
from jax import lax
from jax.experimental import pallas as pl
from jax.experimental.pallas import tpu as pltpu
from jax.sharding import PartitionSpec as P

DECAY = 0.9
EPSILON = 1e-06
MESH = pl.DeviceIdType.MESH
F32 = jnp.float32
BF16 = jnp.bfloat16
SLOTS = 3
PLANES = 8
ROWMATES = 16
MEMBERS = 4
VIA_RIGHT = 64


def one_hot(condition):
    return jnp.where(condition, 1.0, 0.0).astype(BF16)


def iota(shape, dim):
    return lax.broadcasted_iota(jnp.int32, shape, dim)


def dot(a, b, contract=((1,), (0,))):
    return lax.dot_general(a, b, (contract, ((), ())), preferred_element_type=F32)


def across(row, tall):
    return jnp.concatenate(
        [one_hot(tall == row[:, 128 * t : 128 * t + 128]) for t in range(row.shape[1] // 128)], axis=1
    )


def sorted_block(index):
    slot, rowmate, plane = index >> 7, (index >> 3) & 15, index & 7
    return (plane * ROWMATES + rowmate) * SLOTS + slot


def kernel(
    grads_in, owner_in, left_stat, right_stat, left_root, right_root,
    new_left, new_right, precond,
    grads, owner, l_stat, r_stat, target, by_row, blocks, spread, stage,
    send_a, recv_a, send_b, g, roots, full, root_relay_0, root_relay_1, p, send_c, recv_c, send_d, recv_d, total,
    outer_send, outer_recv, outer_relay_0, outer_relay_1,
    local_sem, a_send, a_recv, b_send, b_recv, c_send, c_recv, d_send, d_recv,
    root_send, root_recv, root_relay_recv, outer_sent, outer_arrived, outer_relay_recv, members_in,
):
    d = lax.axis_index("dp")
    c = lax.axis_index("mp")
    plane = d // ROWMATES
    mate = d % ROWMATES
    right = lax.rem(c + 1, MEMBERS)
    left = lax.rem(c + MEMBERS - 1, MEMBERS)
    far = lax.rem(c + 2, MEMBERS)
    to_right, to_left = (d, right), (d, left)

    twice = 2 * lax.rem(d, 2)
    shift = lax.rem(twice + plane, MEMBERS)
    own_slot, right_slot, far_slot, left_slot = [lax.rem(c + i + MEMBERS - shift, MEMBERS) for i in range(MEMBERS)]

    def worker(k, owner_plane):
        return lax.rem(k + twice + owner_plane, MEMBERS)

    def far_first(j, count):
        return count // 2 + (j // 2) * (2 * (j % 2) - 1)

    def mate_at(j):
        other = lax.rem(mate + far_first(j, ROWMATES), ROWMATES)
        return other, plane * ROWMATES + other

    def plane_at(j):
        other = lax.rem(plane + far_first(j, PLANES), PLANES)
        return other, other * ROWMATES + mate

    def remote(src, dst, send, recv, device):
        return pltpu.make_async_remote_copy(
            src_ref=src, dst_ref=dst, send_sem=send, recv_sem=recv, device_id=device, device_id_type=MESH
        )

    def wait_bytes(ref, sem):
        pltpu.make_async_copy(ref, ref, sem).wait()

    def aligned(start, size):
        return pl.ds(pl.multiple_of(start, size), size)

    own = [
        pltpu.make_async_copy(owner_in, owner, local_sem.at[5]),
        pltpu.make_async_copy(grads_in, grads, local_sem.at[0]),
        pltpu.make_async_copy(left_root, roots.at[0], local_sem.at[1]),
        pltpu.make_async_copy(right_root, roots.at[1], local_sem.at[2]),
        pltpu.make_async_copy(left_stat, l_stat, local_sem.at[3]),
        pltpu.make_async_copy(right_stat, r_stat, local_sem.at[4]),
    ]
    for copy in own:
        copy.start()

    barrier = pltpu.get_barrier_semaphore()

    @pl.loop(1, ROWMATES, unroll=True)
    def _(j):
        pl.semaphore_signal(barrier, inc=1, device_id=(mate_at(j)[1], c), device_id_type=MESH)

    @pl.loop(1, MEMBERS, unroll=True)
    def _(j):
        pl.semaphore_signal(barrier, inc=1, device_id=(d, lax.rem(c + j, MEMBERS)), device_id_type=MESH)

    @pl.loop(1, PLANES, unroll=True)
    def _(j):
        pl.semaphore_signal(barrier, inc=1, device_id=(plane_at(j)[1], c), device_id_type=MESH)

    pl.semaphore_wait(barrier, ROWMATES + MEMBERS + PLANES - 3)

    def tell_column():
        @pl.loop(1, PLANES, unroll=True)
        def _(j):
            pl.semaphore_signal(members_in, inc=1, device_id=(plane_at(j)[1], c), device_id_type=MESH)

    top, bottom = pl.ds(0, VIA_RIGHT), pl.ds(VIA_RIGHT, 128 - VIA_RIGHT)

    def start_roots():
        @pl.when(far_slot < SLOTS)
        def _():
            remote(
                roots.at[:, far_slot, top], root_relay_0, root_send.at[2], root_relay_recv.at[0], to_right
            ).start()
            remote(
                roots.at[:, far_slot, bottom], root_relay_1, root_send.at[3], root_relay_recv.at[1], to_left
            ).start()

        @pl.when(right_slot < SLOTS)
        def _():
            remote(roots.at[:, right_slot], full.at[:, c], root_send.at[0], root_recv, to_right).start()

        @pl.when(left_slot < SLOTS)
        def _():
            remote(roots.at[:, left_slot], full.at[:, c], root_send.at[1], root_recv, to_left).start()

        @pl.when(own_slot < SLOTS)
        def _():
            full[:, c] = roots[:, own_slot]

    def pass_roots():
        @pl.when(right_slot < SLOTS)
        def _():
            wait_bytes(root_relay_0, root_relay_recv.at[0])
            remote(root_relay_0, full.at[:, left, top], root_send.at[4], root_recv, to_right).start()

        @pl.when(left_slot < SLOTS)
        def _():
            wait_bytes(root_relay_1, root_relay_recv.at[1])
            remote(root_relay_1, full.at[:, right, bottom], root_send.at[5], root_recv, to_left).start()

    def start_a(k):
        wanted = sorted_block(iota((128, 128), 0) + 128 * k).astype(F32)
        moved = dot(across(target[0:1, :], wanted), blocks[...])
        rows = [moved[:, 128 * i : 128 * i + 128].reshape(ROWMATES, 1, PLANES, 128) for i in range(4)]
        send_a[k] = jnp.concatenate(rows, axis=1).reshape(ROWMATES, 32, 128).astype(BF16)

        @pl.loop(1, ROWMATES, unroll=True)
        def _(j):
            other, device = mate_at(j)
            remote(send_a.at[k, other], recv_a.at[k, mate], a_send.at[k], a_recv.at[k], (device, c)).start()

        recv_a[k, mate] = send_a[k, mate]

    def start_b(k):
        wait_bytes(recv_a.at[k, pl.ds(0, ROWMATES - 1)], a_recv.at[k])
        stage[...] = recv_a[k].reshape(512, 128).astype(F32)
        for i in range(PLANES):
            send_b[k, i] = stage[pl.ds(i, 64, stride=PLANES), :].astype(BF16)
        member = worker(k, plane)
        place = c * PLANES + plane

        @pl.loop(1, PLANES, unroll=True)
        def _(j):
            other, device = plane_at(j)
            remote(send_b.at[k, other], g.at[place], b_send.at[k], b_recv, (device, worker(k, other))).start()

        @pl.when(member != c)
        def _():
            remote(send_b.at[k, plane], g.at[place], b_send.at[k], b_recv, (d, member)).start()

        @pl.when(member == c)
        def _():
            g[place] = send_b[k, plane]

    def gradient():
        parts = [g[pl.ds(PLANES * j, PLANES)].reshape(512, 128) for j in range(MEMBERS)]
        return jnp.concatenate(parts, axis=1)

    def work():
        wait_bytes(full.at[:, pl.ds(0, MEMBERS - 1)], root_recv)
        wait_bytes(g.at[pl.ds(0, PLANES * MEMBERS - 1)], b_recv)
        wide = gradient()
        half_way = dot(wide, full[1].reshape(512, 512)).astype(BF16)
        p[...] = dot(full[0].reshape(512, 512), half_way)
        grad_squares = jnp.zeros((1, 512), F32)
        product_squares = jnp.zeros((1, 512), F32)
        for i in range(4):
            part = wide[128 * i : 128 * i + 128].astype(F32)
            grad_squares = grad_squares + jnp.sum(part * part, axis=0, keepdims=True)
            part = p[pl.ds(128 * i, 128), :]
            product_squares = product_squares + jnp.sum(part * part, axis=0, keepdims=True)
        grad_squares = jnp.sum(grad_squares, axis=1, keepdims=True)
        product_squares = jnp.sum(product_squares, axis=1, keepdims=True)
        scale = jnp.sqrt(grad_squares / (product_squares + EPSILON))
        for j in range(MEMBERS):
            send_c[j] = (p[:, 128 * j : 128 * j + 128] * scale).astype(BF16).reshape(PLANES, 64, 128)

        def send(member, other):
            remote(
                send_c.at[member, other], recv_c.at[own_slot, plane],
                c_send, c_recv.at[own_slot], (other * ROWMATES + mate, member),
            ).start()

        @pl.loop(0, (PLANES - 1) * MEMBERS, unroll=True)
        def _(j):
            send(lax.rem(c + 2 + j % MEMBERS, MEMBERS), plane_at(j // MEMBERS + 1)[0])

        @pl.loop(1, MEMBERS, unroll=True)
        def _(j):
            send(lax.rem(c + j, MEMBERS), plane)

        recv_c[own_slot, plane] = send_c[c, plane]

    def outer_products():
        wide = gradient()
        outer_send[0] = dot(wide, wide, ((1,), (1,))).astype(BF16).reshape(MEMBERS, 128, 512)
        outer_send[1] = dot(wide, wide, ((0,), (0,))).astype(BF16).reshape(MEMBERS, 128, 512)
        remote(
            outer_send.at[:, far, top], outer_relay_0, outer_sent.at[2], outer_relay_recv.at[0], to_right
        ).start()
        remote(
            outer_send.at[:, far, bottom], outer_relay_1, outer_sent.at[3], outer_relay_recv.at[1], to_left
        ).start()
        for number, (member, device) in enumerate(((right, to_right), (left, to_left))):
            remote(
                outer_send.at[:, member], outer_recv.at[own_slot],
                outer_sent.at[number], outer_arrived.at[own_slot], device,
            ).start()
        outer_recv[own_slot] = outer_send[:, c]

    def pass_outer(k):
        @pl.when(left_slot == k)
        def _():
            wait_bytes(outer_relay_0, outer_relay_recv.at[0])
            remote(
                outer_relay_0, outer_recv.at[k, :, top],
                outer_sent.at[4], outer_arrived.at[k], to_right,
            ).start()

        @pl.when(right_slot == k)
        def _():
            wait_bytes(outer_relay_1, outer_relay_recv.at[1])
            remote(
                outer_relay_1, outer_recv.at[k, :, bottom],
                outer_sent.at[5], outer_arrived.at[k], to_left,
            ).start()

    def statistics(k):
        @pl.when(worker(k, plane) != c)
        def _():
            wait_bytes(outer_recv.at[k], outer_arrived.at[k])

        new_left[k] = DECAY * l_stat[k] + (1.0 - DECAY) / 512 * outer_recv[k, 0].astype(F32)
        new_right[k] = DECAY * r_stat[k] + (1.0 - DECAY) / 512 * outer_recv[k, 1].astype(F32)

    def start_d(k):
        @pl.when(worker(k, plane) != c)
        def _():
            wait_bytes(recv_c.at[k], c_recv.at[k])

        @pl.when(worker(k, plane) == c)
        def _():
            wait_bytes(recv_c.at[k, pl.ds(0, PLANES - 1)], c_recv.at[k])

        for i in range(PLANES):
            stage[pl.ds(i, 64, stride=PLANES), :] = recv_c[k, i].astype(F32)
        send_d[k] = stage[...].astype(BF16).reshape(ROWMATES, 32, 128)

        @pl.loop(1, ROWMATES, unroll=True)
        def _(j):
            other, device = mate_at(j)
            remote(send_d.at[k, other], recv_d.at[k, mate], d_send.at[k], d_recv.at[k], (device, c)).start()

        recv_d[k, mate] = send_d[k, mate]

    def finish(k):
        wait_bytes(recv_d.at[k, pl.ds(0, ROWMATES - 1)], d_recv.at[k])
        pieces = recv_d[k].astype(F32).reshape(ROWMATES, 4, PLANES, 128)
        pieces = jnp.concatenate([pieces[:, i].reshape(128, 128) for i in range(4)], axis=1).astype(BF16)
        part = dot(spread[:, 128 * k : 128 * k + 128], pieces)
        if k > 0:
            part = part + total[...]
        if k < SLOTS - 1:
            total[...] = part
        else:
            for i in range(4):
                by_row[pl.ds(i, 384, stride=4), :] = part[:, 128 * i : 128 * i + 128]
            precond[...] = by_row[...].astype(BF16)

    own[2].wait()
    own[3].wait()
    start_roots()

    own[0].wait()
    owned = jnp.concatenate([one_hot(owner[i : i + 1, :] == iota((128, 128), 0)) for i in range(3)], axis=1)
    earlier = iota((128, 384), 0).astype(F32) * SLOTS
    for i in range(3):
        earlier += dot(
            owned[:, 128 * i : 128 * i + 128], one_hot(iota((128, 384), 0) + 128 * i < iota((128, 384), 1))
        )
    number = jnp.sum(owned.astype(F32) * earlier, axis=0, keepdims=True)
    target[...] = jnp.broadcast_to(number, (8, 384))

    own[1].wait()
    by_row[...] = grads[...].astype(F32)
    for i in range(4):
        blocks[:, 128 * i : 128 * i + 128] = by_row[pl.ds(i, 384, stride=4), :].astype(BF16)
    start_a(0)
    tell_column()
    start_a(1)
    start_a(2)
    column = jnp.transpose(jnp.broadcast_to(target[0:1, :], (128, 384)))
    spread[...] = across(sorted_block(iota((1, 384), 1)).astype(F32), column)

    pl.semaphore_wait(members_in, PLANES - 1)
    start_b(0)
    pass_roots()
    start_b(1)
    start_b(2)
    for copy in own[4:]:
        copy.wait()
    pl.when(own_slot < SLOTS)(work)
    pl.when(own_slot < SLOTS)(outer_products)
    start_d(0)
    pass_outer(0)
    start_d(1)
    pass_outer(1)
    start_d(2)
    pass_outer(2)
    finish(0)
    finish(1)
    statistics(0)
    statistics(1)
    finish(2)
    statistics(2)

    for k in range(SLOTS):
        wait_bytes(send_a.at[k, pl.ds(0, ROWMATES - 1)], a_send.at[k])
        wait_bytes(send_d.at[k, pl.ds(0, ROWMATES - 1)], d_send.at[k])

        @pl.when(worker(k, plane) != c)
        def _():
            wait_bytes(send_b.at[k], b_send.at[k])

        @pl.when(worker(k, plane) == c)
        def _():
            wait_bytes(send_b.at[k, pl.ds(0, PLANES - 1)], b_send.at[k])

    @pl.when(own_slot < SLOTS)
    def _():
        wait_bytes(g.at[pl.ds(0, PLANES * MEMBERS - 1)], c_send)
        for i in range(2):
            wait_bytes(outer_recv.at[0], outer_sent.at[i])
        wait_bytes(outer_relay_0, outer_sent.at[2])
        wait_bytes(outer_relay_1, outer_sent.at[3])

    @pl.when(right_slot < SLOTS)
    def _():
        wait_bytes(full.at[:, 0], root_send.at[0])
        wait_bytes(root_relay_0, root_send.at[4])
        wait_bytes(outer_relay_1, outer_sent.at[5])

    @pl.when(left_slot < SLOTS)
    def _():
        wait_bytes(full.at[:, 0], root_send.at[1])
        wait_bytes(root_relay_1, root_send.at[5])
        wait_bytes(outer_relay_0, outer_sent.at[4])

    @pl.when(far_slot < SLOTS)
    def _():
        wait_bytes(root_relay_0, root_send.at[2])
        wait_bytes(root_relay_1, root_send.at[3])


def copy_kernel(*refs):
    sources, results, sem = refs[:3], refs[3:6], refs[6]
    copies = []
    for source, result in zip(sources, results):
        third = source.shape[0] // 3
        for i in range(3):
            rows = pl.ds(i * third, third)
            copies.append(pltpu.make_async_copy(source.at[rows], result.at[rows], sem.at[len(copies)]))
    for copy in copies:
        copy.start()
    for copy in copies:
        copy.wait()


def local(grads, owner, left_stat, right_stat, left_root, right_root):
    any_space = pl.BlockSpec(memory_space=pl.ANY)
    vmem = pl.BlockSpec(memory_space=pltpu.VMEM)
    dma = pltpu.SemaphoreType.DMA
    shapes = (
        jax.ShapeDtypeStruct((3, 128, 512), F32),
        jax.ShapeDtypeStruct((3, 128, 512), F32),
        jax.ShapeDtypeStruct((1536, 128), BF16),
    )
    results = pl.pallas_call(
        kernel,
        out_shape=tuple(pltpu.VMEM(x.shape, x.dtype) for x in shapes),
        in_specs=[any_space] * 6,
        out_specs=(vmem,) * 3,
        scratch_shapes=[
            pltpu.VMEM((1536, 128), BF16),
            pltpu.VMEM((3, 128), jnp.int32),
            pltpu.VMEM((3, 128, 512), F32),
            pltpu.VMEM((3, 128, 512), F32),
            pltpu.VMEM((8, 384), F32),
            pltpu.VMEM((1536, 128), F32),
            pltpu.VMEM((384, 512), BF16),
            pltpu.VMEM((384, 384), BF16),
            pltpu.VMEM((512, 128), F32),
            pltpu.VMEM((3, 16, 32, 128), BF16),
            pltpu.VMEM((3, 16, 32, 128), BF16),
            pltpu.VMEM((3, 8, 64, 128), BF16),
            pltpu.VMEM((32, 64, 128), BF16),
            pltpu.VMEM((2, 3, 128, 512), BF16),
            pltpu.VMEM((2, 4, 128, 512), BF16),
            pltpu.VMEM((2, VIA_RIGHT, 512), BF16),
            pltpu.VMEM((2, 128 - VIA_RIGHT, 512), BF16),
            pltpu.VMEM((512, 512), F32),
            pltpu.VMEM((4, 8, 64, 128), BF16),
            pltpu.VMEM((3, 8, 64, 128), BF16),
            pltpu.VMEM((3, 16, 32, 128), BF16),
            pltpu.VMEM((3, 16, 32, 128), BF16),
            pltpu.VMEM((384, 512), F32),
            pltpu.VMEM((2, 4, 128, 512), BF16),
            pltpu.VMEM((3, 2, 128, 512), BF16),
            pltpu.VMEM((2, VIA_RIGHT, 512), BF16),
            pltpu.VMEM((2, 128 - VIA_RIGHT, 512), BF16),
            dma((6,)),
            dma((3,)), dma((3,)),
            dma((3,)), dma,
            dma, dma((3,)),
            dma((3,)), dma((3,)),
            dma((6,)), dma, dma((2,)),
            dma((6,)), dma((3,)), dma((2,)),
            pltpu.SemaphoreType.REGULAR,
        ],
        compiler_params=pltpu.CompilerParams(
            collective_id=0, has_side_effects=True, vmem_limit_bytes=58 * 1024 * 1024
        ),
        cost_estimate=pl.CostEstimate(flops=4_000_000_000, bytes_accessed=6_000_000, transcendentals=0),
    )(grads.reshape(1536, 128), owner.reshape(3, 128), left_stat, right_stat, left_root, right_root)
    new_left, new_right, precond = pl.pallas_call(
        copy_kernel,
        out_shape=shapes,
        in_specs=[vmem] * 3,
        out_specs=(any_space,) * 3,
        scratch_shapes=[dma((9,))],
        compiler_params=pltpu.CompilerParams(vmem_limit_bytes=4 * 1024 * 1024),
        cost_estimate=pl.CostEstimate(flops=0, bytes_accessed=4_000_000, transcendentals=0),
    )(*results)
    return new_left, new_right, precond.reshape(384, 4, 128)


def solution(mesh):
    in_specs = (
        P(None, "dp", "mp"),
        P(),
        P("dp", "mp", None),
        P("dp", "mp", None),
        P("dp", "mp", None),
        P("dp", "mp", None),
    )
    out_specs = (P("dp", "mp", None), P("dp", "mp", None), P(None, "dp", "mp"))
    return jax.shard_map(local, mesh=mesh, in_specs=in_specs, out_specs=out_specs, check_vma=False)
```

time: 183 us -> 54.5 us (0.30)
  waiting for transfers between devices: 83.4 us -> 0 us
  Pallas kernels: 0 us -> 53.7 us
  blocking collectives: 43.9 us -> 0 us
  starting transfers between devices: 15.3 us -> 0 us
  between operations: 13.9 us -> 0.64 us
  other arithmetic: 12.9 us -> 0 us
  local copies, waits for them, and re-layouts: 7.45 us -> 0 us
  matrix products: 6.37 us -> 0 us
    all_gather x3 -> x0, waiting for transfers between devices: 65 us -> none  [the longest x1 33.1 us: local(): whole_rows = lax.all_gather(finished, 'mp', axis=1, tiled=True)]
    pallas_call x0 -> x2, Pallas kernels: none -> 53.7 us  [the longest x1 52.4 us: local(): pl.pallas_call(kernel, out_shape=tuple((pltpu.VMEM(x.shape, x.dtype) for...]
    all_to_all x1 -> x0, blocking collectives: 36.1 us -> none  [local(): lax.all_to_all(sorted_pieces, 'dp', split_axis=0, concat_axis=1, tiled=True)]
    all_to_all x1 -> x0, waiting for transfers between devices: 17.7 us -> none  [local(): lax.all_to_all(column_slice, 'dp', split_axis=1, concat_axis=0, tiled=True)]
    all_to_all x1 -> x0, starting transfers between devices: 15.2 us -> none  [local(): lax.all_to_all(column_slice, 'dp', split_axis=1, concat_axis=0, tiled=True)]
    sort x2 -> x0, other arithmetic: 8.22 us -> none  [the longest x1 4.45 us: local(): slot_order = jnp.argsort(owner, stable=True)]
    psum x1 -> x0, blocking collectives: 7.75 us -> none  [local(): product_squares = lax.psum(jnp.sum(product * product, axis=(1, 2)), 'mp')]
    dot_general x3 -> x0, matrix products: 6.37 us -> none  [the longest x1 3.52 us: local(): jnp.einsum('orb,obc->orc', left_root, half_way, preferred_element_type=jn...]
  transfers between devices with their start and end apart: 4 -> 0, of which waited for: 3 -> 0; matrix products, arithmetic and copies ran while one was open for 8% -> 0% of each run, Pallas kernels for 0% -> 0%
where the time goes in v1:
time: 54.5 us; the launch traced here: 54.3 us
  Pallas kernels  53.7 us (99%)
  between operations  0.64 us (1%)
    pallas_call x1, Pallas kernels, local(): pl.pallas_call(kernel, out_shape=tuple((pltpu.VMEM(x.shape, x.dtype) for...  52.4 us
    pallas_call x1, Pallas kernels, local(): pl.pallas_call(copy_kernel, out_shape=shapes, in_specs=[vmem] * 3, out_sp...  1.34 us

profile of v1, /device:TPU:1, one launch (start us, length us, event | category | flops | bytes accessed | tf_op | source)
XLA Modules:
  0.0 54.3 jit_solution(17284561508187270703)
XLA Ops:
  0.6 52.4 %shard_map.85 = (f32[3,128,512]{2,1,0:T(8,128)S(1)}, f32[3,128,512]{2,1,0:T(8,128)S(1)}, bf16[1536,128]{1,0:T(8,128)(2,1)S(1)}) custom-call(bf16[1536,128]{1,0:T(8,128)(2,1)} %bitcast.3, s32[3,128]{1,0:T(4,128)} %bitcast.5, f32[3,128,512]{2,1,0:T(8,128)} %left_stat.1, f32[3,128,512]{2,1,0:T(8,128)} %right_stat.1, bf16[3,128,512]{2,1,0:T(8,128)(2,1)} %left_root.1, ...), custom_call_target="tpu_custom_call" | custom-call | flops 4000000000 | bytes 6000000 | tf_op jit(solution)/shard_map/pallas_call | solution.py:414
  53.0 1.3 %shard_map.86 = (f32[3,128,512]{2,1,0:T(8,128)}, f32[3,128,512]{2,1,0:T(8,128)}, bf16[1536,128]{1,0:T(8,128)(2,1)}) custom-call(f32[3,128,512]{2,1,0:T(8,128)S(1)} %get-tuple-element.9.refs_0_, f32[3,128,512]{2,1,0:T(8,128)S(1)} %get-tuple-element.10.refs_1_, bf16[1536,128]{1,0:T(8,128)(2,1)S(1)} %get-tuple-element.11.refs_2_), custom_call_target="tpu_custom_call" | custom-call | bytes 4000000 | tf_op jit(solution)/shard_map/pallas_call | solution.py:461

commit v2 on v1

--- a/solution.py
+++ b/solution.py
@@ -40,11 +40,16 @@
     return (plane * ROWMATES + rowmate) * SLOTS + slot
 
 
+def side_by_side(pieces):
+    rows = pieces.astype(F32).reshape(ROWMATES, 4, PLANES, 128)
+    return jnp.concatenate([rows[:, i].reshape(128, 128) for i in range(4)], axis=1).astype(BF16)
+
+
 def kernel(
     grads_in, owner_in, left_stat, right_stat, left_root, right_root,
-    new_left, new_right, precond,
+    new_left, new_right, total, last_spread, last_pieces,
     grads, owner, l_stat, r_stat, target, by_row, blocks, spread, stage,
-    send_a, recv_a, send_b, g, roots, full, root_relay_0, root_relay_1, p, send_c, recv_c, send_d, recv_d, total,
+    send_a, recv_a, send_b, g, roots, full, root_relay_0, root_relay_1, p, send_c, recv_c, send_d, recv_d,
     outer_send, outer_recv, outer_relay_0, outer_relay_1,
     local_sem, a_send, a_recv, b_send, b_recv, c_send, c_recv, d_send, d_recv,
     root_send, root_recv, root_relay_recv, outer_sent, outer_arrived, outer_relay_recv, members_in,
@@ -95,7 +100,7 @@
         pltpu.make_async_copy(left_stat, l_stat, local_sem.at[3]),
         pltpu.make_async_copy(right_stat, r_stat, local_sem.at[4]),
     ]
-    for copy in own:
+    for copy in own[:2]:
         copy.start()
 
     barrier = pltpu.get_barrier_semaphore()
@@ -112,7 +117,8 @@
     def _(j):
         pl.semaphore_signal(barrier, inc=1, device_id=(plane_at(j)[1], c), device_id_type=MESH)
 
-    pl.semaphore_wait(barrier, ROWMATES + MEMBERS + PLANES - 3)
+    for copy in own[2:]:
+        copy.start()
 
     def tell_column():
         @pl.loop(1, PLANES, unroll=True)
@@ -154,12 +160,13 @@
             wait_bytes(root_relay_1, root_relay_recv.at[1])
             remote(root_relay_1, full.at[:, right, bottom], root_send.at[5], root_recv, to_left).start()
 
-    def start_a(k):
+    def make_a(k):
         wanted = sorted_block(iota((128, 128), 0) + 128 * k).astype(F32)
         moved = dot(across(target[0:1, :], wanted), blocks[...])
         rows = [moved[:, 128 * i : 128 * i + 128].reshape(ROWMATES, 1, PLANES, 128) for i in range(4)]
         send_a[k] = jnp.concatenate(rows, axis=1).reshape(ROWMATES, 32, 128).astype(BF16)
 
+    def start_a(k):
         @pl.loop(1, ROWMATES, unroll=True)
         def _(j):
             other, device = mate_at(j)
@@ -291,21 +298,8 @@
 
     def finish(k):
         wait_bytes(recv_d.at[k, pl.ds(0, ROWMATES - 1)], d_recv.at[k])
-        pieces = recv_d[k].astype(F32).reshape(ROWMATES, 4, PLANES, 128)
-        pieces = jnp.concatenate([pieces[:, i].reshape(128, 128) for i in range(4)], axis=1).astype(BF16)
-        part = dot(spread[:, 128 * k : 128 * k + 128], pieces)
-        if k > 0:
-            part = part + total[...]
-        if k < SLOTS - 1:
-            total[...] = part
-        else:
-            for i in range(4):
-                by_row[pl.ds(i, 384, stride=4), :] = part[:, 128 * i : 128 * i + 128]
-            precond[...] = by_row[...].astype(BF16)
-
-    own[2].wait()
-    own[3].wait()
-    start_roots()
+        part = dot(spread[:, 128 * k : 128 * k + 128], side_by_side(recv_d[k]))
+        total[...] = part if k == 0 else part + total[...]
 
     own[0].wait()
     owned = jnp.concatenate([one_hot(owner[i : i + 1, :] == iota((128, 128), 0)) for i in range(3)], axis=1)
@@ -321,10 +315,16 @@
     by_row[...] = grads[...].astype(F32)
     for i in range(4):
         blocks[:, 128 * i : 128 * i + 128] = by_row[pl.ds(i, 384, stride=4), :].astype(BF16)
+    make_a(0)
+    pl.semaphore_wait(barrier, ROWMATES + MEMBERS + PLANES - 3)
     start_a(0)
     tell_column()
-    start_a(1)
-    start_a(2)
+    own[2].wait()
+    own[3].wait()
+    start_roots()
+    for k in (1, 2):
+        make_a(k)
+        start_a(k)
     column = jnp.transpose(jnp.broadcast_to(target[0:1, :], (128, 384)))
     spread[...] = across(sorted_block(iota((1, 384), 1)).astype(F32), column)
 
@@ -347,7 +347,9 @@
     finish(1)
     statistics(0)
     statistics(1)
-    finish(2)
+    last_spread[...] = spread[:, 256:384]
+    wait_bytes(recv_d.at[2, pl.ds(0, ROWMATES - 1)], d_recv.at[2])
+    last_pieces[...] = recv_d[2]
     statistics(2)
 
     for k in range(SLOTS):
@@ -388,16 +390,22 @@
         wait_bytes(root_relay_1, root_send.at[3])
 
 
-def copy_kernel(*refs):
-    sources, results, sem = refs[:3], refs[3:6], refs[6]
-    copies = []
-    for source, result in zip(sources, results):
-        third = source.shape[0] // 3
-        for i in range(3):
-            rows = pl.ds(i * third, third)
-            copies.append(pltpu.make_async_copy(source.at[rows], result.at[rows], sem.at[len(copies)]))
+def last_kernel(
+    new_left, new_right, total, last_spread, last_pieces, left_out, right_out, precond_out, by_row, precond, sem
+):
+    copies = [
+        pltpu.make_async_copy(source.at[k], result.at[k], sem.at[3 * i + k])
+        for i, (source, result) in enumerate(((new_left, left_out), (new_right, right_out)))
+        for k in range(SLOTS)
+    ]
     for copy in copies:
         copy.start()
+    blocks = total[...] + dot(last_spread[...], side_by_side(last_pieces[...]))
+    for i in range(4):
+        by_row[pl.ds(i, 384, stride=4), :] = blocks[:, 128 * i : 128 * i + 128]
+    precond[...] = by_row[...].astype(BF16)
+    copies.append(pltpu.make_async_copy(precond, precond_out, sem.at[6]))
+    copies[-1].start()
     for copy in copies:
         copy.wait()
 
@@ -406,16 +414,17 @@
     any_space = pl.BlockSpec(memory_space=pl.ANY)
     vmem = pl.BlockSpec(memory_space=pltpu.VMEM)
     dma = pltpu.SemaphoreType.DMA
-    shapes = (
-        jax.ShapeDtypeStruct((3, 128, 512), F32),
-        jax.ShapeDtypeStruct((3, 128, 512), F32),
-        jax.ShapeDtypeStruct((1536, 128), BF16),
-    )
     results = pl.pallas_call(
         kernel,
-        out_shape=tuple(pltpu.VMEM(x.shape, x.dtype) for x in shapes),
+        out_shape=(
+            pltpu.VMEM((3, 128, 512), F32),
+            pltpu.VMEM((3, 128, 512), F32),
+            pltpu.VMEM((384, 512), F32),
+            pltpu.VMEM((384, 128), BF16),
+            pltpu.VMEM((16, 32, 128), BF16),
+        ),
         in_specs=[any_space] * 6,
-        out_specs=(vmem,) * 3,
+        out_specs=(vmem,) * 5,
         scratch_shapes=[
             pltpu.VMEM((1536, 128), BF16),
             pltpu.VMEM((3, 128), jnp.int32),
@@ -439,7 +448,6 @@
             pltpu.VMEM((3, 8, 64, 128), BF16),
             pltpu.VMEM((3, 16, 32, 128), BF16),
             pltpu.VMEM((3, 16, 32, 128), BF16),
-            pltpu.VMEM((384, 512), F32),
             pltpu.VMEM((2, 4, 128, 512), BF16),
             pltpu.VMEM((3, 2, 128, 512), BF16),
             pltpu.VMEM((2, VIA_RIGHT, 512), BF16),
@@ -459,11 +467,15 @@
         cost_estimate=pl.CostEstimate(flops=4_000_000_000, bytes_accessed=6_000_000, transcendentals=0),
     )(grads.reshape(1536, 128), owner.reshape(3, 128), left_stat, right_stat, left_root, right_root)
     new_left, new_right, precond = pl.pallas_call(
-        copy_kernel,
-        out_shape=shapes,
-        in_specs=[vmem] * 3,
+        last_kernel,
+        out_shape=(
+            jax.ShapeDtypeStruct((3, 128, 512), F32),
+            jax.ShapeDtypeStruct((3, 128, 512), F32),
+            jax.ShapeDtypeStruct((1536, 128), BF16),
+        ),
+        in_specs=[vmem] * 5,
         out_specs=(any_space,) * 3,
-        scratch_shapes=[dma((9,))],
+        scratch_shapes=[pltpu.VMEM((1536, 128), F32), pltpu.VMEM((1536, 128), BF16), dma((7,))],
         compiler_params=pltpu.CompilerParams(vmem_limit_bytes=4 * 1024 * 1024),
         cost_estimate=pl.CostEstimate(flops=0, bytes_accessed=4_000_000, transcendentals=0),
     )(*results)

time: 54.5 us -> 54.7 us (level)
  no operation moved by 1% of the time
where the time goes in v2:
time: 54.7 us; the launch traced here: 54.6 us
  Pallas kernels  54 us (99%)
  between operations  0.64 us (1%)
    pallas_call x1, Pallas kernels, local(): pl.pallas_call(kernel, out_shape=(pltpu.VMEM((3, 128, 512), F32), pltpu.V...  52.6 us
    pallas_call x1, Pallas kernels, local(): pl.pallas_call(last_kernel, out_shape=(jax.ShapeDtypeStruct((3, 128, 512)...  1.33 us

profile of v2, /device:TPU:1, one launch (start us, length us, event | category | flops | bytes accessed | tf_op | source)
XLA Modules:
  0.0 54.6 jit_solution(16677890209165045231)
XLA Ops:
  0.6 52.6 %shard_map.85 = (f32[3,128,512]{2,1,0:T(8,128)S(1)}, f32[3,128,512]{2,1,0:T(8,128)S(1)}, f32[384,512]{1,0:T(8,128)S(1)}, bf16[384,128]{1,0:T(8,128)(2,1)S(1)}, bf16[16,32,128]{2,1,0:T(8,128)(2,1)S(1)}) custom-call(bf16[1536,128]{1,0:T(8,128)(2,1)} %bitcast.3, s32[3,128]{1,0:T(4,128)} %bitcast.5, f32[3,128,512]{2,1,0:T(8,128)} %left_stat.1, ...), custom_call_target="tpu_custom_call" | custom-call | flops 4000000000 | bytes 6000000 | tf_op jit(solution)/shard_map/pallas_call | solution.py:417
  53.3 1.3 %shard_map.86 = (f32[3,128,512]{2,1,0:T(8,128)}, f32[3,128,512]{2,1,0:T(8,128)}, bf16[1536,128]{1,0:T(8,128)(2,1)}) custom-call(f32[3,128,512]{2,1,0:T(8,128)S(1)} %get-tuple-element.11.new_left, f32[3,128,512]{2,1,0:T(8,128)S(1)} %get-tuple-element.12.new_right, f32[384,512]{1,0:T(8,128)S(1)} %get-tuple-element.13.total, ...), custom_call_target="tpu_custom_call" | custom-call | bytes 4000000 | tf_op jit(solution)/shard_map/pallas_call | solution.py:469

commit v3 on v2

--- a/solution.py
+++ b/solution.py
@@ -316,12 +316,12 @@
     for i in range(4):
         blocks[:, 128 * i : 128 * i + 128] = by_row[pl.ds(i, 384, stride=4), :].astype(BF16)
     make_a(0)
+    own[2].wait()
+    own[3].wait()
     pl.semaphore_wait(barrier, ROWMATES + MEMBERS + PLANES - 3)
+    start_roots()
     start_a(0)
     tell_column()
-    own[2].wait()
-    own[3].wait()
-    start_roots()
     for k in (1, 2):
         make_a(k)
         start_a(k)
@@ -336,13 +336,13 @@
     for copy in own[4:]:
         copy.wait()
     pl.when(own_slot < SLOTS)(work)
-    pl.when(own_slot < SLOTS)(outer_products)
+    pl.when(own_slot == SLOTS - 1)(outer_products)
     start_d(0)
-    pass_outer(0)
     start_d(1)
-    pass_outer(1)
+    pl.when(own_slot < SLOTS - 1)(outer_products)
     start_d(2)
-    pass_outer(2)
+    for k in range(SLOTS):
+        pass_outer(k)
     finish(0)
     finish(1)
     statistics(0)

time: 54.7 us -> 55.7 us (1.018); the launches traced: 54.6 us -> 54.6 us
  no operation moved by 1% of the time
where the time goes in v3:
time: 55.7 us; the launch traced here: 54.6 us
  Pallas kernels  54 us (97%)
  between operations  0.64 us (1%)
    pallas_call x1, Pallas kernels, local(): pl.pallas_call(kernel, out_shape=(pltpu.VMEM((3, 128, 512), F32), pltpu.V...  52.7 us
    pallas_call x1, Pallas kernels, local(): pl.pallas_call(last_kernel, out_shape=(jax.ShapeDtypeStruct((3, 128, 512)...  1.33 us

profile of v3, /device:TPU:1, one launch (start us, length us, event | category | flops | bytes accessed | tf_op | source)
XLA Modules:
  0.0 54.6 jit_solution(18290243179002436063)
XLA Ops:
  0.6 52.7 %shard_map.85 = (f32[3,128,512]{2,1,0:T(8,128)S(1)}, f32[3,128,512]{2,1,0:T(8,128)S(1)}, f32[384,512]{1,0:T(8,128)S(1)}, bf16[384,128]{1,0:T(8,128)(2,1)S(1)}, bf16[16,32,128]{2,1,0:T(8,128)(2,1)S(1)}) custom-call(bf16[1536,128]{1,0:T(8,128)(2,1)} %bitcast.3, s32[3,128]{1,0:T(4,128)} %bitcast.5, f32[3,128,512]{2,1,0:T(8,128)} %left_stat.1, ...), custom_call_target="tpu_custom_call" | custom-call | flops 4000000000 | bytes 6000000 | tf_op jit(solution)/shard_map/pallas_call | solution.py:417
  53.3 1.3 %shard_map.86 = (f32[3,128,512]{2,1,0:T(8,128)}, f32[3,128,512]{2,1,0:T(8,128)}, bf16[1536,128]{1,0:T(8,128)(2,1)}) custom-call(f32[3,128,512]{2,1,0:T(8,128)S(1)} %get-tuple-element.11.new_left, f32[3,128,512]{2,1,0:T(8,128)S(1)} %get-tuple-element.12.new_right, f32[384,512]{1,0:T(8,128)S(1)} %get-tuple-element.13.total, ...), custom_call_target="tpu_custom_call" | custom-call | bytes 4000000 | tf_op jit(solution)/shard_map/pallas_call | solution.py:469

commit v4 on v3

--- a/solution.py
+++ b/solution.py
@@ -11,6 +11,7 @@
 F32 = jnp.float32
 BF16 = jnp.bfloat16
 SLOTS = 3
+HALVES = 2
 PLANES = 8
 ROWMATES = 16
 MEMBERS = 4
@@ -218,19 +219,22 @@
         for j in range(MEMBERS):
             send_c[j] = (p[:, 128 * j : 128 * j + 128] * scale).astype(BF16).reshape(PLANES, 64, 128)
 
-        def send(member, other):
-            remote(
-                send_c.at[member, other], recv_c.at[own_slot, plane],
-                c_send, c_recv.at[own_slot], (other * ROWMATES + mate, member),
-            ).start()
-
-        @pl.loop(0, (PLANES - 1) * MEMBERS, unroll=True)
-        def _(j):
-            send(lax.rem(c + 2 + j % MEMBERS, MEMBERS), plane_at(j // MEMBERS + 1)[0])
-
-        @pl.loop(1, MEMBERS, unroll=True)
-        def _(j):
-            send(lax.rem(c + j, MEMBERS), plane)
+        for half in range(HALVES):
+            rows = pl.ds(32 * half, 32)
+
+            def send(member, other):
+                remote(
+                    send_c.at[member, other, rows], recv_c.at[own_slot, plane, rows],
+                    c_send, c_recv.at[own_slot, half], (other * ROWMATES + mate, member),
+                ).start()
+
+            @pl.loop(0, (PLANES - 1) * MEMBERS, unroll=True)
+            def _(j):
+                send(lax.rem(c + 2 + j % MEMBERS, MEMBERS), plane_at(j // MEMBERS + 1)[0])
+
+            @pl.loop(1, MEMBERS, unroll=True)
+            def _(j):
+                send(lax.rem(c + j, MEMBERS), plane)
 
         recv_c[own_slot, plane] = send_c[c, plane]
 
@@ -277,22 +281,29 @@
         new_right[k] = DECAY * r_stat[k] + (1.0 - DECAY) / 512 * outer_recv[k, 1].astype(F32)
 
     def start_d(k):
-        @pl.when(worker(k, plane) != c)
-        def _():
-            wait_bytes(recv_c.at[k], c_recv.at[k])
-
-        @pl.when(worker(k, plane) == c)
-        def _():
-            wait_bytes(recv_c.at[k, pl.ds(0, PLANES - 1)], c_recv.at[k])
-
-        for i in range(PLANES):
-            stage[pl.ds(i, 64, stride=PLANES), :] = recv_c[k, i].astype(F32)
-        send_d[k] = stage[...].astype(BF16).reshape(ROWMATES, 32, 128)
-
-        @pl.loop(1, ROWMATES, unroll=True)
-        def _(j):
-            other, device = mate_at(j)
-            remote(send_d.at[k, other], recv_d.at[k, mate], d_send.at[k], d_recv.at[k], (device, c)).start()
+        for half in range(HALVES):
+            rows = pl.ds(32 * half, 32)
+
+            @pl.when(worker(k, plane) != c)
+            def _():
+                wait_bytes(recv_c.at[k, :, rows], c_recv.at[k, half])
+
+            @pl.when(worker(k, plane) == c)
+            def _():
+                wait_bytes(recv_c.at[k, pl.ds(0, PLANES - 1), rows], c_recv.at[k, half])
+
+            for i in range(PLANES):
+                stage[pl.ds(i, 32, stride=PLANES), :] = recv_c[k, i, rows].astype(F32)
+            send_d[k, pl.ds(8 * half, 8)] = stage[pl.ds(0, 256), :].astype(BF16).reshape(8, 32, 128)
+
+            @pl.loop(0, 8, unroll=True)
+            def _(j):
+                other = 8 * half + lax.rem(mate + 4 + j, 8)
+
+                @pl.when(other != mate)
+                def _():
+                    device = (plane * ROWMATES + other, c)
+                    remote(send_d.at[k, other], recv_d.at[k, mate], d_send.at[k], d_recv.at[k], device).start()
 
         recv_d[k, mate] = send_d[k, mate]
 
@@ -336,12 +347,9 @@
     for copy in own[4:]:
         copy.wait()
     pl.when(own_slot < SLOTS)(work)
-    pl.when(own_slot == SLOTS - 1)(outer_products)
-    start_d(0)
-    start_d(1)
-    pl.when(own_slot < SLOTS - 1)(outer_products)
-    start_d(2)
+    pl.when(own_slot < SLOTS)(outer_products)
     for k in range(SLOTS):
+        start_d(k)
         pass_outer(k)
     finish(0)
     finish(1)
@@ -455,7 +463,7 @@
             dma((6,)),
             dma((3,)), dma((3,)),
             dma((3,)), dma,
-            dma, dma((3,)),
+            dma, dma((3, 2)),
             dma((3,)), dma((3,)),
             dma((6,)), dma, dma((2,)),
             dma((6,)), dma((3,)), dma((2,)),

time: 55.7 us -> 54.7 us (0.982); the launches traced: 54.6 us -> 54.6 us
  no operation moved by 1% of the time
where the time goes in v4:
time: 54.7 us; the launch traced here: 54.6 us
  Pallas kernels  53.9 us (99%)
  between operations  0.64 us (1%)
    pallas_call x1, Pallas kernels, local(): pl.pallas_call(kernel, out_shape=(pltpu.VMEM((3, 128, 512), F32), pltpu.V...  52.6 us
    pallas_call x1, Pallas kernels, local(): pl.pallas_call(last_kernel, out_shape=(jax.ShapeDtypeStruct((3, 128, 512)...  1.33 us

profile of v4, /device:TPU:1, one launch (start us, length us, event | category | flops | bytes accessed | tf_op | source)
XLA Modules:
  0.0 54.6 jit_solution(957592497107571567)
XLA Ops:
  0.6 52.6 %shard_map.85 = (f32[3,128,512]{2,1,0:T(8,128)S(1)}, f32[3,128,512]{2,1,0:T(8,128)S(1)}, f32[384,512]{1,0:T(8,128)S(1)}, bf16[384,128]{1,0:T(8,128)(2,1)S(1)}, bf16[16,32,128]{2,1,0:T(8,128)(2,1)S(1)}) custom-call(bf16[1536,128]{1,0:T(8,128)(2,1)} %bitcast.3, s32[3,128]{1,0:T(4,128)} %bitcast.5, f32[3,128,512]{2,1,0:T(8,128)} %left_stat.1, ...), custom_call_target="tpu_custom_call" | custom-call | flops 4000000000 | bytes 6000000 | tf_op jit(solution)/shard_map/pallas_call | solution.py:425
  53.2 1.3 %shard_map.86 = (f32[3,128,512]{2,1,0:T(8,128)}, f32[3,128,512]{2,1,0:T(8,128)}, bf16[1536,128]{1,0:T(8,128)(2,1)}) custom-call(f32[3,128,512]{2,1,0:T(8,128)S(1)} %get-tuple-element.11.new_left, f32[3,128,512]{2,1,0:T(8,128)S(1)} %get-tuple-element.12.new_right, f32[384,512]{1,0:T(8,128)S(1)} %get-tuple-element.13.total, ...), custom_call_target="tpu_custom_call" | custom-call | bytes 4000000 | tf_op jit(solution)/shard_map/pallas_call | solution.py:477

commit v5 on v4

--- a/solution.py
+++ b/solution.py
@@ -15,7 +15,7 @@
 PLANES = 8
 ROWMATES = 16
 MEMBERS = 4
-VIA_RIGHT = 64
+VIA_RIGHT = 32
 
 
 def one_hot(condition):
@@ -339,9 +339,9 @@
     column = jnp.transpose(jnp.broadcast_to(target[0:1, :], (128, 384)))
     spread[...] = across(sorted_block(iota((1, 384), 1)).astype(F32), column)
 
+    pass_roots()
     pl.semaphore_wait(members_in, PLANES - 1)
     start_b(0)
-    pass_roots()
     start_b(1)
     start_b(2)
     for copy in own[4:]:

time: 54.7 us -> 56.4 us (1.031)
  Pallas kernels: 53.9 us -> 55.6 us
    pallas_call x1, Pallas kernels: 52.6 us -> 54.2 us  [local(): pl.pallas_call(kernel, out_shape=(pltpu.VMEM((3, 128, 512), F32), pltpu.V...]
where the time goes in v5:
time: 56.4 us; the launch traced here: 56.2 us
  Pallas kernels  55.6 us (99%)
  between operations  0.64 us (1%)
    pallas_call x1, Pallas kernels, local(): pl.pallas_call(kernel, out_shape=(pltpu.VMEM((3, 128, 512), F32), pltpu.V...  54.2 us
    pallas_call x1, Pallas kernels, local(): pl.pallas_call(last_kernel, out_shape=(jax.ShapeDtypeStruct((3, 128, 512)...  1.33 us

profile of v5, /device:TPU:1, one launch (start us, length us, event | category | flops | bytes accessed | tf_op | source)
XLA Modules:
  0.0 56.2 jit_solution(12251350446091888986)
XLA Ops:
  0.6 54.2 %shard_map.85 = (f32[3,128,512]{2,1,0:T(8,128)S(1)}, f32[3,128,512]{2,1,0:T(8,128)S(1)}, f32[384,512]{1,0:T(8,128)S(1)}, bf16[384,128]{1,0:T(8,128)(2,1)S(1)}, bf16[16,32,128]{2,1,0:T(8,128)(2,1)S(1)}) custom-call(bf16[1536,128]{1,0:T(8,128)(2,1)} %bitcast.3, s32[3,128]{1,0:T(4,128)} %bitcast.5, f32[3,128,512]{2,1,0:T(8,128)} %left_stat.1, ...), custom_call_target="tpu_custom_call" | custom-call | flops 4000000000 | bytes 6000000 | tf_op jit(solution)/shard_map/pallas_call | solution.py:425
  54.9 1.3 %shard_map.86 = (f32[3,128,512]{2,1,0:T(8,128)}, f32[3,128,512]{2,1,0:T(8,128)}, bf16[1536,128]{1,0:T(8,128)(2,1)}) custom-call(f32[3,128,512]{2,1,0:T(8,128)S(1)} %get-tuple-element.11.new_left, f32[3,128,512]{2,1,0:T(8,128)S(1)} %get-tuple-element.12.new_right, f32[384,512]{1,0:T(8,128)S(1)} %get-tuple-element.13.total, ...), custom_call_target="tpu_custom_call" | custom-call | bytes 4000000 | tf_op jit(solution)/shard_map/pallas_call | solution.py:477

commit v6 on v4

--- a/solution.py
+++ b/solution.py
@@ -128,35 +128,35 @@
 
     top, bottom = pl.ds(0, VIA_RIGHT), pl.ds(VIA_RIGHT, 128 - VIA_RIGHT)
 
-    def start_roots():
-        @pl.when(far_slot < SLOTS)
+    def start_roots(k):
+        @pl.when(far_slot == k)
         def _():
             remote(
-                roots.at[:, far_slot, top], root_relay_0, root_send.at[2], root_relay_recv.at[0], to_right
+                roots.at[:, k, top], root_relay_0, root_send.at[2], root_relay_recv.at[0], to_right
             ).start()
             remote(
-                roots.at[:, far_slot, bottom], root_relay_1, root_send.at[3], root_relay_recv.at[1], to_left
+                roots.at[:, k, bottom], root_relay_1, root_send.at[3], root_relay_recv.at[1], to_left
             ).start()
 
-        @pl.when(right_slot < SLOTS)
-        def _():
-            remote(roots.at[:, right_slot], full.at[:, c], root_send.at[0], root_recv, to_right).start()
-
-        @pl.when(left_slot < SLOTS)
-        def _():
-            remote(roots.at[:, left_slot], full.at[:, c], root_send.at[1], root_recv, to_left).start()
-
-        @pl.when(own_slot < SLOTS)
-        def _():
-            full[:, c] = roots[:, own_slot]
-
-    def pass_roots():
-        @pl.when(right_slot < SLOTS)
+        @pl.when(right_slot == k)
+        def _():
+            remote(roots.at[:, k], full.at[:, c], root_send.at[0], root_recv, to_right).start()
+
+        @pl.when(left_slot == k)
+        def _():
+            remote(roots.at[:, k], full.at[:, c], root_send.at[1], root_recv, to_left).start()
+
+        @pl.when(own_slot == k)
+        def _():
+            full[:, c] = roots[:, k]
+
+    def pass_roots(k):
+        @pl.when(right_slot == k)
         def _():
             wait_bytes(root_relay_0, root_relay_recv.at[0])
             remote(root_relay_0, full.at[:, left, top], root_send.at[4], root_recv, to_right).start()
 
-        @pl.when(left_slot < SLOTS)
+        @pl.when(left_slot == k)
         def _():
             wait_bytes(root_relay_1, root_relay_recv.at[1])
             remote(root_relay_1, full.at[:, right, bottom], root_send.at[5], root_recv, to_left).start()
@@ -330,20 +330,20 @@
     own[2].wait()
     own[3].wait()
     pl.semaphore_wait(barrier, ROWMATES + MEMBERS + PLANES - 3)
-    start_roots()
+    start_roots(0)
     start_a(0)
     tell_column()
     for k in (1, 2):
+        start_roots(k)
         make_a(k)
         start_a(k)
     column = jnp.transpose(jnp.broadcast_to(target[0:1, :], (128, 384)))
     spread[...] = across(sorted_block(iota((1, 384), 1)).astype(F32), column)
 
     pl.semaphore_wait(members_in, PLANES - 1)
-    start_b(0)
-    pass_roots()
-    start_b(1)
-    start_b(2)
+    for k in range(SLOTS):
+        start_b(k)
+        pass_roots(k)
     for copy in own[4:]:
         copy.wait()
     pl.when(own_slot < SLOTS)(work)

time: 54.7 us -> 53.9 us (0.985)
  Pallas kernels: 53.9 us -> 53.1 us
    pallas_call x1, Pallas kernels: 52.6 us -> 51.8 us  [local(): pl.pallas_call(kernel, out_shape=(pltpu.VMEM((3, 128, 512), F32), pltpu.V...]
where the time goes in v6:
time: 53.9 us; the launch traced here: 53.8 us
  Pallas kernels  53.1 us (99%)
  between operations  0.64 us (1%)
    pallas_call x1, Pallas kernels, local(): pl.pallas_call(kernel, out_shape=(pltpu.VMEM((3, 128, 512), F32), pltpu.V...  51.8 us
    pallas_call x1, Pallas kernels, local(): pl.pallas_call(last_kernel, out_shape=(jax.ShapeDtypeStruct((3, 128, 512)...  1.33 us

profile of v6, /device:TPU:1, one launch (start us, length us, event | category | flops | bytes accessed | tf_op | source)
XLA Modules:
  0.0 53.8 jit_solution(16164153272894568797)
XLA Ops:
  0.6 51.8 %shard_map.85 = (f32[3,128,512]{2,1,0:T(8,128)S(1)}, f32[3,128,512]{2,1,0:T(8,128)S(1)}, f32[384,512]{1,0:T(8,128)S(1)}, bf16[384,128]{1,0:T(8,128)(2,1)S(1)}, bf16[16,32,128]{2,1,0:T(8,128)(2,1)S(1)}) custom-call(bf16[1536,128]{1,0:T(8,128)(2,1)} %bitcast.3, s32[3,128]{1,0:T(4,128)} %bitcast.5, f32[3,128,512]{2,1,0:T(8,128)} %left_stat.1, ...), custom_call_target="tpu_custom_call" | custom-call | flops 4000000000 | bytes 6000000 | tf_op jit(solution)/shard_map/pallas_call | solution.py:425
  52.4 1.3 %shard_map.86 = (f32[3,128,512]{2,1,0:T(8,128)}, f32[3,128,512]{2,1,0:T(8,128)}, bf16[1536,128]{1,0:T(8,128)(2,1)}) custom-call(f32[3,128,512]{2,1,0:T(8,128)S(1)} %get-tuple-element.11.new_left, f32[3,128,512]{2,1,0:T(8,128)S(1)} %get-tuple-element.12.new_right, f32[384,512]{1,0:T(8,128)S(1)} %get-tuple-element.13.total, ...), custom_call_target="tpu_custom_call" | custom-call | bytes 4000000 | tf_op jit(solution)/shard_map/pallas_call | solution.py:477

commit v7 on v6

--- a/solution.py
+++ b/solution.py
@@ -240,19 +240,19 @@
 
     def outer_products():
         wide = gradient()
-        outer_send[0] = dot(wide, wide, ((1,), (1,))).astype(BF16).reshape(MEMBERS, 128, 512)
-        outer_send[1] = dot(wide, wide, ((0,), (0,))).astype(BF16).reshape(MEMBERS, 128, 512)
-        remote(
-            outer_send.at[:, far, top], outer_relay_0, outer_sent.at[2], outer_relay_recv.at[0], to_right
-        ).start()
-        remote(
-            outer_send.at[:, far, bottom], outer_relay_1, outer_sent.at[3], outer_relay_recv.at[1], to_left
-        ).start()
-        for number, (member, device) in enumerate(((right, to_right), (left, to_left))):
+        for i, axis in enumerate((1, 0)):
+            outer_send[i] = dot(wide, wide, ((axis,), (axis,))).astype(BF16).reshape(MEMBERS, 128, 512)
             remote(
-                outer_send.at[:, member], outer_recv.at[own_slot],
-                outer_sent.at[number], outer_arrived.at[own_slot], device,
+                outer_send.at[i, far, top], outer_relay_0.at[i], outer_sent.at[2], outer_relay_recv.at[0], to_right
             ).start()
+            remote(
+                outer_send.at[i, far, bottom], outer_relay_1.at[i], outer_sent.at[3], outer_relay_recv.at[1], to_left
+            ).start()
+            for number, (member, device) in enumerate(((right, to_right), (left, to_left))):
+                remote(
+                    outer_send.at[i, member], outer_recv.at[own_slot, i],
+                    outer_sent.at[number], outer_arrived.at[own_slot], device,
+                ).start()
         outer_recv[own_slot] = outer_send[:, c]
 
     def pass_outer(k):

time: 53.9 us -> 53.9 us (level)
  no operation moved by 1% of the time
where the time goes in v7:
time: 53.9 us; the launch traced here: 53.8 us
  Pallas kernels  53.1 us (99%)
  between operations  0.64 us (1%)
    pallas_call x1, Pallas kernels, local(): pl.pallas_call(kernel, out_shape=(pltpu.VMEM((3, 128, 512), F32), pltpu.V...  51.8 us
    pallas_call x1, Pallas kernels, local(): pl.pallas_call(last_kernel, out_shape=(jax.ShapeDtypeStruct((3, 128, 512)...  1.33 us

profile of v7, /device:TPU:1, one launch (start us, length us, event | category | flops | bytes accessed | tf_op | source)
XLA Modules:
  0.0 53.8 jit_solution(7234413361713003932)
XLA Ops:
  0.6 51.8 %shard_map.85 = (f32[3,128,512]{2,1,0:T(8,128)S(1)}, f32[3,128,512]{2,1,0:T(8,128)S(1)}, f32[384,512]{1,0:T(8,128)S(1)}, bf16[384,128]{1,0:T(8,128)(2,1)S(1)}, bf16[16,32,128]{2,1,0:T(8,128)(2,1)S(1)}) custom-call(bf16[1536,128]{1,0:T(8,128)(2,1)} %bitcast.3, s32[3,128]{1,0:T(4,128)} %bitcast.5, f32[3,128,512]{2,1,0:T(8,128)} %left_stat.1, ...), custom_call_target="tpu_custom_call" | custom-call | flops 4000000000 | bytes 6000000 | tf_op jit(solution)/shard_map/pallas_call | solution.py:425
  52.4 1.3 %shard_map.86 = (f32[3,128,512]{2,1,0:T(8,128)}, f32[3,128,512]{2,1,0:T(8,128)}, bf16[1536,128]{1,0:T(8,128)(2,1)}) custom-call(f32[3,128,512]{2,1,0:T(8,128)S(1)} %get-tuple-element.11.new_left, f32[3,128,512]{2,1,0:T(8,128)S(1)} %get-tuple-element.12.new_right, f32[384,512]{1,0:T(8,128)S(1)} %get-tuple-element.13.total, ...), custom_call_target="tpu_custom_call" | custom-call | bytes 4000000 | tf_op jit(solution)/shard_map/pallas_call | solution.py:477
